TPU v7x, 256 devices: a whole 4x4x8 slice. The times are simulated.
256 devices in a mesh: wide: 32 (over x, y, core), narrow: 8 (over z).
Axes of the slice: x: 4, y: 4, z: 8, core: 2. Of those that a mesh axis runs over, the one named last changes fastest.
Arguments:
- hidden: bfloat16 [4096, 4096], P('wide', 'narrow'), may hold values from -6 to 6
- head_weight: bfloat16 [131072, 4096], P('wide', 'narrow'), may hold values from -0.25 to 0.25
- lse: float32 [4096], replicated, may hold values from 12 to 14
- targets: int32 [4096], replicated, may hold values from 0 to 131071
- loss_weight: float32 [4096], replicated, may hold values from 16 to 48
- block_tiles: int32 [32, 32, 4], P(None, 'wide'), may hold values from 0 to 31, as said below
- block_counts: int32 [32, 32], P(None, 'wide'), may hold values from 0 to 4, as said below
- gate_pre: bfloat16 [4096, 7168], P('wide', 'narrow'), may hold values from -6 to 6
- up_pre: bfloat16 [4096, 7168], P('wide', 'narrow'), may hold values from -6 to 6
- down_weight: bfloat16 [7168, 4096], P('narrow'), may hold values from -0.0625 to 0.0625
Outputs:
- head_grad: bfloat16 [4096, 4096], P('wide', 'narrow')
- gate_grad: bfloat16 [4096, 7168], P('wide', 'narrow')
- up_grad: bfloat16 [4096, 7168], P('wide', 'narrow')
Inputs may be any that keep to these rules, and one draw needn't show every extreme that they name: The first block_counts[b, s] entries of block_tiles[b, s] are distinct; the other entries are ignored. `block_counts`: some row block has 4 active tiles in some shard; one shard has exactly 64 active tiles over all row blocks, and no shard has more.
All inputs are finite; a program needn't handle non-finite values.
Results may differ from a plain program's by a relative error of at most 0.0035.
The roundings to bfloat16 on the way count: a program that leaves them out, or rounds other values in their place, can miss the bound.
Values may be sent and summed in bfloat16 or wider, within the bound.
A program may use at most 128 MiB of HBM per device.

v0:
```python
import jax
import jax.numpy as jnp
from jax import lax
from jax.sharding import PartitionSpec as P

TILE = 128


def sent_to_all(x, axis):
    copies = jnp.broadcast_to(x, (lax.axis_size(axis), *x.shape))
    return lax.all_to_all(copies, axis, split_axis=0, concat_axis=0, tiled=True)


def in_order(pieces, dim):
    pieces = jnp.moveaxis(pieces, 0, dim)
    lengths = pieces.shape
    return pieces.reshape(*lengths[:dim], lengths[dim] * lengths[dim + 1], *lengths[dim + 2 :])


def collect(x, axis, dim):
    pieces = sent_to_all(x, axis)
    return in_order(pieces, dim)


def slot_table(tiles_here, counts_here, slot_count):
    block_total, per_block = tiles_here.shape
    slot_live = (jnp.arange(per_block, dtype=jnp.int32)[None, :] < counts_here[:, None]).reshape(-1)
    position = jnp.cumsum(slot_live.astype(jnp.int32)) - 1
    select = (position[None, :] == jnp.arange(slot_count, dtype=jnp.int32)[:, None]) & slot_live[
        None, :
    ]
    chosen = select.astype(jnp.int32)
    block_ids = jnp.repeat(jnp.arange(block_total, dtype=jnp.int32), per_block)
    slot_blocks = jnp.sum(chosen * block_ids[None, :], axis=1)
    slot_tiles = jnp.sum(chosen * tiles_here.reshape(-1)[None, :], axis=1)
    return (slot_blocks, slot_tiles, jnp.sum(chosen, axis=1) > 0)


def cell_weights(logits, lse_rows, scale_rows, slot_live):
    scaled = jnp.exp(logits - lse_rows[:, :, None]) * scale_rows[:, :, None]
    return jnp.where(slot_live[:, None, None], scaled, 0.0).astype(jnp.bfloat16)


def on_device(
    hidden,
    head_weight,
    lse,
    targets,
    loss_weight,
    block_tiles,
    block_counts,
    gate_pre,
    up_pre,
    down_weight,
):
    features = hidden.shape[1]
    row_count = hidden.shape[0]
    vocab_here = head_weight.shape[0]
    offset = lax.axis_index("wide") * vocab_here
    gathered = lax.all_gather(hidden, "wide", axis=0, tiled=True)
    blocks = gathered.shape[0] // TILE
    weight_tiles = head_weight.reshape(vocab_here // TILE, TILE, features)
    tiles_here = block_tiles[:, 0, :]
    counts_here = block_counts[:, 0]
    per_block = tiles_here.shape[1]
    lse_blocks = lse.reshape(blocks, TILE)
    scale_blocks = loss_weight.reshape(blocks, TILE)
    slot_count = blocks // 2 * per_block
    slot_blocks, slot_tiles, slot_live = slot_table(tiles_here, counts_here, slot_count)
    picked = jnp.take(weight_tiles, slot_tiles, axis=0)
    row_blocks = jnp.take(gathered.reshape(blocks, TILE, features), slot_blocks, axis=0)
    partial_value = jnp.einsum(
        "srd,scd->src", row_blocks, picked, preferred_element_type=jnp.float32
    )
    slot_lse = jnp.take(lse_blocks, slot_blocks, axis=0)
    slot_scale = jnp.take(scale_blocks, slot_blocks, axis=0)
    shared = lax.psum_scatter(partial_value, "narrow", scatter_dimension=1, tiled=True)
    part_rows = shared.shape[1]
    first_row = lax.axis_index("narrow") * part_rows
    part_lse = lax.dynamic_slice_in_dim(slot_lse, first_row, part_rows, 1)
    part_scale = lax.dynamic_slice_in_dim(slot_scale, first_row, part_rows, 1)
    part_probs = cell_weights(shared, part_lse, part_scale, slot_live)
    cell_probs = lax.all_gather(part_probs, "narrow", axis=1, tiled=True)
    contrib = jnp.einsum("src,scd->srd", cell_probs, picked, preferred_element_type=jnp.float32)
    contrib = contrib.reshape(slot_count, TILE * features)
    block_span = row_count * lax.axis_size("wide") // TILE
    wanted = jnp.arange(block_span, dtype=jnp.int32)
    member = ((slot_blocks[None, :] == wanted[:, None]) & slot_live[None, :]).astype(jnp.float32)
    softmax_part = jnp.dot(
        member, contrib, precision=lax.Precision.HIGHEST, preferred_element_type=jnp.float32
    ).reshape(row_count * lax.axis_size("wide"), features)
    local_ids = targets - offset
    inside = (local_ids >= 0) & (local_ids < vocab_here)
    target_rows = jnp.take(head_weight, jnp.clip(local_ids, 0, vocab_here - 1), axis=0).astype(
        jnp.float32
    )
    factor = jnp.where(inside, loss_weight, 0.0)
    head_grad = lax.psum_scatter(
        softmax_part - factor[:, None] * target_rows, "wide", scatter_dimension=0, tiled=True
    ).astype(jnp.bfloat16)
    unit_grad = lax.dot_general(
        collect(head_grad, "narrow", 1),
        down_weight,
        (((1,), (1,)), ((), ())),
        preferred_element_type=jnp.float32,
    )
    gate_value = gate_pre.astype(jnp.float32)
    up_value = up_pre.astype(jnp.float32)
    gate_sig = jax.nn.sigmoid(gate_value)
    up_grad = (unit_grad * gate_value * gate_sig).astype(jnp.bfloat16)
    gate_grad = (unit_grad * up_value * gate_sig * (1.0 + gate_value * (1.0 - gate_sig))).astype(
        jnp.bfloat16
    )
    return (head_grad, gate_grad, up_grad)


def solution(mesh):
    in_specs = (
        P("wide", "narrow"),
        P("wide", "narrow"),
        P(),
        P(),
        P(),
        P(None, "wide", None),
        P(None, "wide"),
        P("wide", "narrow"),
        P("wide", "narrow"),
        P("narrow", None),
    )
    out_specs = (P("wide", "narrow"), P("wide", "narrow"), P("wide", "narrow"))
    return jax.shard_map(
        on_device, mesh=mesh, in_specs=in_specs, out_specs=out_specs, check_vma=False
    )
```

profile of v0, /device:TPU:2, one launch (start us, length us, event | category | flops | bytes accessed | tf_op | source)
XLA Modules:
  0.0 381.3 jit_solution(11211163191481606287)
XLA Ops:
  7.2 0.7 all-gather.3.cloned.1.call-update
  8.0 0.7 iota_compare_fusion.2
  8.8 0.1 lt.65
  8.9 0.1 mul.60
  9.0 0.8 copy.19
  9.8 0.1 mul.63
  9.9 0.2 reduce-window.8
  10.0 0.1 add_reduce_fusion
  10.2 0.2 convert_reduce_fusion
  10.3 7.7 %gather_fusion.2 = bf16[64,128,512]{2,1,0:T(8,128)(2,1)} fusion(bf16[32,128,512]{2,1,0:T(8,128)(2,1)} %bitcast.17, s32[1024]{0:T(1024)S(1)} %pad_clamp_fusion), kind=kCustom, calls=%fused_computation.2.clone | custom fusion | bytes 16777472 | tf_op jit(solution)/shard_map/jit(_take)/gather | solution.py:70
  18.1 46.3 %all-gather.3.cloned.1.call-done = bf16[4096,512]{1,0:T(8,128)(2,1)} async-done(((bf16[128,512]{1,0:T(8,128)(2,1)}), bf16[4096,512]{1,0:T(8,128)(2,1)}) %all-gather.3.cloned.1.call-update) | async-done | bytes 4194320 | tf_op jit(solution)/shard_map/all_gather | solution.py:60
  64.3 7.7 %gather_fusion.1 = bf16[64,128,512]{2,1,0:T(8,128)(2,1)} fusion(bf16[32,128,512]{2,1,0:T(8,128)(2,1)} %bitcast.20, s32[1024]{0:T(1024)S(1)} %pad_clamp_fusion.1), kind=kCustom, calls=%fused_computation.clone | custom fusion | bytes 16777472 | tf_op jit(solution)/shard_map/jit(_take)/gather | solution.py:71
  72.1 10.5 %fusion = f32[64,128,128]{2,1,0:T(8,128)} fusion(bf16[64,128,512]{2,1,0:T(8,128)(2,1)} %gather_fusion.1, pred[64]{0:T(512)(128)(4,1)S(1)} %get-tuple-element.15, bf16[64,128,512]{2,1,0:T(8,128)(2,1)} %gather_fusion.2, pred[64]{0:T(512)(128)(4,1)S(1)} %get-tuple-element.14), kind=kOutput, calls=%fused_computation.5 | convolution fusion | flops 1082130432 | bytes 20971648 | tf_op jit(solution)/shard_map/srd,scd->src/dot_general | solution.py:72
  82.6 0.6 gather_fusion.3
  83.3 0.6 gather_fusion.4
  83.9 0.1 dynamic-slice_select_fusion.1
  84.0 53.8 %reduce-scatter.3.cloned.1.call-done = f32[64,16,128]{2,1,0:T(8,128)} async-done(((f32[64,128,128]{2,1,0:T(8,128)}), f32[64,16,128]{2,1,0:T(8,128)}) %reduce-scatter.3.cloned.1.call-update) | async-done | bytes 524304 | tf_op jit(solution)/shard_map/reduce_scatter | solution.py:77
  137.7 2.2 select_convert_fusion
  139.9 0.2 reduce-scatter.5.cloned.1.call-start
  140.2 20.1 %gather_fusion = bf16[4096,512]{1,0:T(8,128)(2,1)} fusion(bf16[4096,512]{1,0:T(8,128)(2,1)} %param.15, s32[4096]{0:T(1024)S(1)} %fusion.17), kind=kCustom, calls=%fused_computation.4 | custom fusion | bytes 8404992 | tf_op jit(solution)/shard_map/jit(_take)/gather | solution.py:94
  160.3 25.5 %all-gather.5.cloned.1.call-done = bf16[64,128,128]{2,1,0:T(8,128)(2,1)} async-done(((bf16[64,16,128]{2,1,0:T(8,128)(2,1)}), bf16[64,128,128]{2,1,0:T(8,128)(2,1)}) %all-gather.5.cloned.1.call-update) | async-done | bytes 2097168 | tf_op jit(solution)/shard_map/all_gather | solution.py:83
  185.9 6.4 %fusion.4 = f32[64,128,512]{2,1,0:T(8,128)S(1)} fusion(bf16[64,128,128]{2,1,0:T(8,128)(2,1)} %all-gather.5.cloned.1.call-done, bf16[64,128,512]{2,1,0:T(8,128)(2,1)} %gather_fusion.2, pred[64]{0:T(512)(128)(4,1)S(1)} %get-tuple-element.14), kind=kOutput, calls=%fused_computation.11 | convolution fusion | flops 1077936128 | bytes 27263040 | tf_op jit(solution)/shard_map/src,scd->srd/dot_general | solution.py:84
  192.3 11.7 %copy.21 = f32[8,8,128,512]{3,1,2,0:T(8,128)} copy(f32[8,8,128,512]{3,2,1,0:T(8,128)S(1)} %bitcast.18) | data formatting | bytes 33554432
  204.0 12.2 %fusion.15 = f32[32,65536]{1,0:T(8,128)} fusion(f32[64,65536]{1,0:T(8,128)} %bitcast.19, s32[64]{0:T(128)S(1)} %get-tuple-element.7, pred[64]{0:T(512)(128)(4,1)S(1)} %broadcast_compare_fusion), kind=kOutput, calls=%fused_computation.36 | convolution fusion | flops 1610616832 | bytes 25166144 | tf_op jit(solution)/shard_map/dot_general | solution.py:89
  216.3 7.5 %reshape.124 = f32[4096,512]{1,0:T(8,128)} reshape(f32[32,65536]{1,0:T(8,128)} %fusion.15) | data formatting | bytes 16777216 | tf_op jit(solution)/shard_map/reshape | solution.py:91
  223.8 9.8 %multiply_subtract_fusion = f32[4096,512]{1,0:T(8,128)} fusion(f32[4096,512]{1,0:T(8,128)} %reshape.124, bf16[4096,512]{1,0:T(8,128)(2,1)} %gather_fusion, f32[4096]{0:T(1024)S(1)} %and_select_fusion, pred[4096]{0:T(1024)(128)(4,1)S(1)} %compare_and_fusion), kind=kLoop, calls=%fused_computation.7 | loop fusion | flops 8388608 | bytes 20992000 | tf_op jit(solution)/shard_map/sub | solution.py:99
  233.6 99.4 %reduce-scatter.5.cloned.1.call-done = f32[128,512]{1,0:T(8,128)} async-done(((f32[4096,512]{1,0:T(8,128)}), f32[128,512]{1,0:T(8,128)}) %reduce-scatter.5.cloned.1.call-update) | async-done | bytes 262160 | tf_op jit(solution)/shard_map/reduce_scatter | solution.py:98
  333.0 1.0 convert_element_type.45
  334.0 0.1 copy.20
  334.1 0.1 broadcast_in_dim.69
  334.3 34.0 %all_to_all.5 = bf16[8,128,512]{1,2,0:T(8,128)(2,1)S(1)} all-to-all(bf16[8,128,512]{1,2,0:T(8,128)(2,1)S(1)} %broadcast_in_dim.69), channel_id=1, replica_groups=mesh['wide'=32,'narrow'=8] {'narrow'}, dimensions={0} | all-to-all | bytes 2097152 | tf_op jit(solution)/shard_map/all_to_all | solution.py:11
  368.3 6.4 %fusion.12 = (bf16[128,896]{1,0:T(8,128)(2,1)}, bf16[128,896]{1,0:T(8,128)(2,1)}) fusion(bf16[128,896]{1,0:T(8,128)(2,1)S(1)} %copy-done.5, bf16[128,896]{1,0:T(8,128)(2,1)S(1)} %copy-done.6, bf16[128,4096]{0,1:T(8,128)(2,1)S(1)} %bitcast.22, bf16[896,4096]{1,0:T(8,128)(2,1)} %param.23), kind=kOutput, calls=%fused_computation.23 | convolution fusion | flops 941244416 | bytes 9306112 | tf_op jit(solution)/shard_map/dot_general | solution.py:101
  (31 shorter events, 0.4 us)
Async XLA Ops:
  7.2 75.5 %copy-start = (f32[4096]{0:T(1024)S(1)}, f32[4096]{0:T(1024)}, u32[]{:S(2)}) copy-start(f32[4096]{0:T(1024)} %param.16) | copy-start | bytes 49156
  7.2 57.1 %all-gather.3.cloned.1.call-start = ((), (), s32[]{:S(2)}) async-start(), calls=%async_computation.3 | async-start | bytes 4325376 | tf_op jit(solution)/shard_map/all_gather | solution.py:60
  7.9 129.8 %reduce-scatter.3.cloned.1.call-start = ((), (), s32[]{:S(2)}) async-start(), calls=%async_computation.4 | async-start | bytes 4718592 | tf_op jit(solution)/shard_map/reduce_scatter | solution.py:77
  72.0 11.2 %copy-start.2 = (f32[4096]{0:T(1024)S(1)}, f32[4096]{0:T(1024)}, u32[]{:S(2)}) copy-start(f32[4096]{0:T(1024)} %param.18) | copy-start | bytes 49156
  72.1 68.1 %copy-start.4 = (s32[4096]{0:T(1024)S(1)}, s32[4096]{0:T(1024)}, u32[]{:S(2)}) copy-start(s32[4096]{0:T(1024)} %param.17) | copy-start | bytes 49156
  82.6 103.3 %all-gather.5.cloned.1.call-start = ((), (), s32[]{:S(2)}) async-start(), calls=%async_computation.5 | async-start | bytes 2359296 | tf_op jit(solution)/shard_map/all_gather | solution.py:83
  139.9 193.1 %reduce-scatter.5.cloned.1.call-start = ((), (), s32[]{:S(2)}) async-start(), calls=%async_computation.6 | async-start | bytes 8650752 | tf_op jit(solution)/shard_map/reduce_scatter | solution.py:98
  233.6 134.7 %copy-start.5 = (bf16[128,896]{1,0:T(8,128)(2,1)S(1)}, bf16[128,896]{1,0:T(8,128)(2,1)}, u32[]{:S(2)}) copy-start(bf16[128,896]{1,0:T(8,128)(2,1)} %param.21) | copy-start | bytes 688132
  233.6 134.7 %copy-start.6 = (bf16[128,896]{1,0:T(8,128)(2,1)S(1)}, bf16[128,896]{1,0:T(8,128)(2,1)}, u32[]{:S(2)}) copy-start(bf16[128,896]{1,0:T(8,128)(2,1)} %param.22) | copy-start | bytes 688132
  233.6 141.1 %copy-start.1 = (f32[4096]{0:T(1024)S(1)}, f32[4096]{0:T(1024)}, u32[]{:S(2)}) copy-start(f32[4096]{0:T(1024)} %param.16) | copy-start | bytes 49156
  334.0 40.8 %copy-start.3 = (bf16[128,512]{1,0:T(8,128)(2,1)}, bf16[128,512]{1,0:T(8,128)(2,1)S(1)}, u32[]{:S(2)}) copy-start(bf16[128,512]{1,0:T(8,128)(2,1)S(1)} %convert_element_type.45) | copy-start | bytes 393220
Sparse Core Ops, SparseCore 0:
  10.6 53.7 all-gather.2
  82.7 54.9 reduce-scatter.2
  140.0 45.8 all-gather.4
  233.8 99.2 reduce-scatter.4
where the time goes:
time: 382 us; the launch traced here: 381 us
  waiting for transfers between devices  226 us (59%)
  local copies, waits for them, and re-layouts  57.4 us (15%)
  matrix products  35.6 us (9%)
  blocking collectives  34 us (9%)
  other arithmetic  14.3 us (4%)
  between operations  13.9 us (4%)
    reduce_scatter x1, waiting for transfers between devices, on_device(): lax.psum_scatter(softmax_part - factor[:, None] * target_rows, 'wide', sc...  99.4 us
    reduce_scatter x1, waiting for transfers between devices, on_device(): lax.psum_scatter(partial_value, 'narrow', scatter_dimension=1, tiled=True)  53.8 us
    all_gather x1, waiting for transfers between devices, on_device(): gathered = lax.all_gather(hidden, 'wide', axis=0, tiled=True)  46.3 us
    all_to_all x1, blocking collectives, sent_to_all(): return lax.all_to_all(copies, axis, split_axis=0, concat_axis=0, tiled=True)  34 us
    all_gather x1, waiting for transfers between devices, on_device(): cell_probs = lax.all_gather(part_probs, 'narrow', axis=1, tiled=True)  25.5 us
    gather x1, local copies, waits for them, and re-layouts, on_device(): jnp.take(head_weight, jnp.clip(local_ids, 0, vocab_here - 1), axis=0)  20.1 us
    unnamed x16, local copies, waits for them, and re-layouts  12.5 us
    dot_general x1, matrix products, on_device(): jnp.dot(member, contrib, precision=lax.Precision.HIGHEST, preferred_eleme...  12.2 us
  transfers between devices with their start and end apart: 4, of which 4 were waited for; matrix products, arithmetic and copies ran while one was open for 8% of the time, Pallas kernels for 0%

commit v1 on v0

v1 whole, which is shorter than its diff:
```python
import jax
import jax.numpy as jnp
from jax import lax
from jax.experimental import pallas as pl
from jax.experimental.pallas import tpu as pltpu
from jax.sharding import PartitionSpec as P

MESH = pl.DeviceIdType.MESH
F32 = jnp.float32
BF16 = jnp.bfloat16
I16 = jnp.int16
I32 = jnp.int32
TILE = 128
SLOTS = 64
BLOCKS = 32
MAXT = 4
FEAT = 512
HU = 896
VT = 32
Z = 8
HALF = 4
UNIT = HALF * TILE + 16


def scale_exponent(top):
    return jnp.clip(jnp.ceil(jnp.log2(top)), -100.0, 127.0)


def code(value, exponent):
    return jnp.round(value * jnp.exp2(14.875 - exponent)).astype(I32).astype(I16)


def factor_of(exponent16):
    return jnp.exp2(exponent16.astype(I32).astype(F32) - 14.875)


def to_f32(coded):
    return coded.astype(I32).astype(F32)


def body(
    hidden,
    weight,
    lse,
    targets,
    scale,
    tiles,
    counts,
    gate,
    up,
    down,
    hg_out,
    gg_out,
    ug_out,
    hid,
    w,
    dw,
    lp,
    probs,
    acc_own,
    acc_sib,
    sib,
    zs,
    zr,
    s1,
    r1,
    s2,
    r2,
    hg,
    unit,
    lse_rows,
    scale_rows,
    pos,
    slot_block,
    slot_tile,
    local_sem,
    hs_sem,
    hr_sem,
    zs_sem,
    zr_sem,
    ps_sem,
    pr_sem,
    bs_sem,
    br_sem,
    s1s_sem,
    s1r_sem,
    s2s_sem,
    s2r_sem,
    gs_sem,
    gr_sem,
):
    me = lax.axis_index("wide")
    z = lax.axis_index("narrow")
    x = me // 8
    y = (me // 2) % 4
    c = me % 2

    def placed(i, j, core):
        xi = i * (1 - core) + j * core
        yi = j * (1 - core) + i * core
        return ((x + xi) % 4) * 8 + ((y + yi) % 4) * 2 + core

    def at(i, j):
        return placed(i, j, c)

    sibling = (x * 8 + y * 2 + 1 - c, z)
    right = (me, (z + 1) % Z)
    left = (me, (z + Z - 1) % Z)

    def remote(src, dst, send, recv, device):
        return pltpu.make_async_remote_copy(
            src_ref=src, dst_ref=dst, send_sem=send, recv_sem=recv, device_id=device, device_id_type=MESH
        )

    own_copy = pltpu.make_async_copy(hidden, hid.at[me], local_sem.at[0])
    own_copy.start()
    w_copy = pltpu.make_async_copy(weight, w, local_sem.at[1])
    w_copy.start()
    dw_copy = pltpu.make_async_copy(down, dw, local_sem.at[2])
    dw_copy.start()

    barrier = pltpu.get_barrier_semaphore()
    peers = [sibling, right, left]
    peers += [(at(i, 0), z) for i in (1, 2, 3)] + [(at(0, j), z) for j in (1, 2, 3)]
    for peer in peers:
        pl.semaphore_signal(barrier, inc=1, device_id=peer, device_id_type=MESH)
    pl.semaphore_wait(barrier, len(peers))

    sends = []

    def go(copy):
        copy.start()
        sends.append(copy)

    def block_send(src, b, k, device):
        go(remote(src, hid.at[b], hs_sem.at[k], hr_sem.at[b], device))

    def block_wait(b):
        remote(hid.at[b], hid.at[b], hs_sem.at[0], hr_sem.at[b], sibling).wait_recv()

    for i in (1, 3, 2):
        block_send(hidden, me, i - 1, (at(i, 0), z))
    for j in (1, 3, 2):
        block_send(hidden, me, 2 + j, (at(0, j), z))
    block_send(hidden, me, 15, sibling)

    def prefix(b, run):
        pos[b] = run
        return run + counts[b, 0]

    pos[BLOCKS] = lax.fori_loop(0, BLOCKS, prefix, jnp.int32(0))

    def fill(s, carry):
        before = jnp.int32(0)
        for b in range(BLOCKS):
            before = before + jnp.clip(s + 1 - pos[b + 1], 0, 1)
        b = jnp.minimum(before, BLOCKS - 1)
        j = jnp.clip(s - pos[b], 0, MAXT - 1)
        slot_block[s] = b
        slot_tile[s] = jnp.clip(tiles[b, 0, j], 0, VT - 1)
        return carry

    lane = lax.broadcasted_iota(I32, (TILE, TILE), 1)
    first = me * (VT * TILE)

    def target_block(acc, k, b):
        ids = jnp.broadcast_to(targets[pl.ds(b, 1), :] - first, (TILE, TILE)).astype(F32).T.astype(I32)
        total = jnp.zeros((TILE, FEAT), F32)
        for v in range(0, VT, 4):
            hot = jnp.concatenate(
                [jnp.where(ids == lane + (v + u) * TILE, 1.0, 0.0).astype(BF16) for u in range(4)], axis=1
            )
            total = total + jnp.dot(hot, w[v : v + 4].reshape(4 * TILE, FEAT), preferred_element_type=F32)
        weights = jnp.broadcast_to(scale[pl.ds(b, 1), :], (TILE, TILE)).T
        for n in range(FEAT // TILE):
            part = slice(n * TILE, (n + 1) * TILE)
            acc[k, :, part] = -weights * total[:, part]

    def target_blocks(lo, hi):
        def pair(k, carry):
            target_block(acc_sib, k, placed(k // 4, k % 4, 1 - c))
            target_block(acc_own, k, placed(k // 4, k % 4, c))
            return carry

        lax.fori_loop(lo // 2, hi // 2, pair, 0)

    lax.fori_loop(0, SLOTS, fill, 0)
    for b in range(BLOCKS):
        lse_rows[b] = jnp.broadcast_to(lse[b : b + 1, :], (8, TILE))
        scale_rows[b] = jnp.broadcast_to(scale[b : b + 1, :], (8, TILE))
    probs[SLOTS] = jnp.zeros((TILE, TILE), BF16)
    w_copy.wait()
    for i in (1, 3, 2):
        b = at(i, 0)
        block_wait(b)
        for j in (1, 3, 2):
            block_send(hid.at[b], b, 2 + i * 3 + j, (at(0, j), z))
        block_send(hid.at[b], b, 15 + i, sibling)
        target_blocks((i - 1) * 2, i * 2)
    for j in (1, 3, 2):
        for i in (0, 1, 3, 2):
            b = at(i, j)
            block_wait(b)
            block_send(hid.at[b], b, 15 + j * 4 + i, sibling)
    own_copy.wait()
    for k in range(16):
        block_wait(2 * k + 1 - c)

    def logits(chunk):
        def slot(i, carry):
            s = chunk * 8 + i
            rows = hid[slot_block[s]]
            entries = w[slot_tile[s]]
            lp[s] = lax.dot_general(entries, rows, (((1,), (1,)), ((), ())), preferred_element_type=F32)
            return carry

        lax.fori_loop(0, 8, slot, 0, unroll=4)

    row16 = lax.broadcasted_iota(I32, (16, TILE), 0) // 4

    def unit_code(k, chunk, half, arrived):
        base = chunk * 8 + half * HALF
        if arrived is not None:
            factors = factor_of(zr[arrived, HALF * TILE : UNIT, :])

        def slot(i, exps):
            value = lp[base + i]
            if arrived is not None:
                factor = jnp.max(jnp.where(row16 == i, factors, 0.0), axis=0, keepdims=True)
                value = value + to_f32(zr[arrived, pl.ds(pl.multiple_of(i * TILE, TILE), TILE), :]) * factor
            e = scale_exponent(jnp.max(jnp.abs(value), axis=0, keepdims=True))
            zs[k, pl.ds(pl.multiple_of(i * TILE, TILE), TILE), :] = code(value, e)
            return jnp.where(row16 == i, e, exps)

        exps = lax.fori_loop(0, HALF, slot, jnp.zeros((16, TILE), F32))
        zs[k, HALF * TILE : UNIT, :] = exps.astype(I32).astype(I16)

    def unit_index(direction, step, half):
        return direction * 8 + step * 2 + half

    def unit_send(direction, step, half):
        k = unit_index(direction, step, half)
        go(remote(zs.at[k], zr.at[k], zs_sem.at[k], zr_sem.at[k], (right, left)[direction]))

    def unit_wait(direction, step, half):
        k = unit_index(direction, step, half)
        remote(zs.at[k], zr.at[k], zs_sem.at[k], zr_sem.at[k], right).wait_recv()
        return k

    def away(direction, distance):
        return (z + (distance if direction == 0 else Z - distance)) % Z

    logits(away(0, 4))
    for direction in (0, 1):
        unit_code(unit_index(direction, 0, direction), away(0, 4), direction, None)
        unit_send(direction, 0, direction)
    for direction in (0, 1):
        logits(away(direction, 3))
        half = 1 - direction
        unit_code(unit_index(direction, 1, half), away(direction, 3), half, None)
        unit_send(direction, 1, half)
    logits(away(0, 2))
    logits(away(1, 2))
    for step in (1, 2, 3):
        for half in (0, 1):
            for direction in (0, 1):
                h = half if direction == 0 else 1 - half
                if step == 1 and h != direction:
                    continue
                k = unit_wait(direction, step - 1, h)
                unit_code(unit_index(direction, step, h), away(direction, 4 - step), h, k)
                unit_send(direction, step, h)
        if step == 1:
            logits(away(0, 1))
            logits(away(1, 1))
            logits(z)
        target_blocks(4 + step * 2, 6 + step * 2)

    def part_refs(t, chunk, half):
        return probs.at[pl.ds(chunk * 8 + half * HALF, HALF)]

    def p_send(direction, step, half):
        k = unit_index(direction, step, half)
        part = part_refs(step, away(1 - direction, step), half)
        go(remote(part, part, ps_sem.at[k], pr_sem.at[k], (right, left)[direction]))

    def p_wait(direction, step, half):
        k = unit_index(direction, step, half)
        part = part_refs(step, away(1 - direction, step + 1), half)
        remote(part, part, ps_sem.at[k], pr_sem.at[k], right).wait_recv()

    for half in (0, 1):
        ka = unit_wait(0, 3, half)
        kb = unit_wait(1, 3, half)
        fa = factor_of(zr[ka, HALF * TILE : UNIT, :])
        fb = factor_of(zr[kb, HALF * TILE : UNIT, :])

        def prob_slot(i, carry, ka=ka, kb=kb, fa=fa, fb=fb, half=half):
            s = z * 8 + half * HALF + i
            part = pl.ds(pl.multiple_of(i * TILE, TILE), TILE)
            factor_a = jnp.max(jnp.where(row16 == i, fa, 0.0), axis=0, keepdims=True)
            factor_b = jnp.max(jnp.where(row16 == i, fb, 0.0), axis=0, keepdims=True)
            value = lp[s] + to_f32(zr[ka, part, :]) * factor_a + to_f32(zr[kb, part, :]) * factor_b
            b = slot_block[s]
            value = jnp.exp(value - lse_rows[b][0:1, :]) * scale_rows[b][0:1, :]
            probs[s] = value.T.astype(BF16)
            return carry

        lax.fori_loop(0, HALF, prob_slot, 0)
        for direction in (0, 1):
            p_send(direction, 0, half)
    target_blocks(12, 16)
    for step in (1, 2, 3):
        for half in (0, 1):
            for direction in (0, 1):
                h = half if direction == 0 else 1 - half
                p_wait(direction, step - 1, h)
                if step < 3 or h == direction:
                    p_send(direction, step, h)
        target_blocks(12 + step * 4, 16 + step * 4)
    target_blocks(28, 32)
    for direction in (0, 1):
        p_wait(direction, 3, direction)

    def contribution(acc, k, b):
        taken, entries = [], []
        for j in range(MAXT):
            live = jnp.clip(counts[b, 0] - j, 0, 1)
            taken.append(probs[jnp.clip(live * (pos[b] + j) + (1 - live) * SLOTS, 0, SLOTS)])
            entries.append(w[jnp.clip(tiles[b, 0, j], 0, VT - 1)])
        acc[k] = acc[k] + jnp.dot(
            jnp.concatenate(taken, axis=1), jnp.concatenate(entries, axis=0), preferred_element_type=F32
        )

    def sib_copy(k):
        return remote(acc_sib.at[k], sib.at[k], bs_sem.at[k], br_sem.at[k], sibling)

    def for_sibling(k, carry):
        contribution(acc_sib, k, placed(k // 4, k % 4, 1 - c))
        return carry

    lax.fori_loop(0, 16, for_sibling, 0)
    for k in range(16):
        go(sib_copy(k))

    def for_own(k, carry):
        contribution(acc_own, k, placed(k // 4, k % 4, c))
        return carry

    lax.fori_loop(0, 16, for_own, 0)
    for k in range(16):
        sib_copy(k).wait_recv()

    def block_code(dst, k, value):
        e = scale_exponent(jnp.max(jnp.abs(value), axis=0, keepdims=True))
        dst[k, 0:TILE, :] = code(value, e)
        dst[k, TILE : TILE + 16, :] = jnp.broadcast_to(e, (16, FEAT)).astype(I32).astype(I16)

    def block_decode(src, k):
        factor = factor_of(src[k, TILE : TILE + 16, :])[0:1, :]
        return to_f32(src[k, 0:TILE, :]) * factor

    def first_copy(i, j):
        k = (j - 1) * 4 + i
        return remote(s1.at[k], r1.at[k], s1s_sem.at[k], s1r_sem.at[k], (at(0, j), z))

    def second_copy(i):
        return remote(s2.at[i - 1], r2.at[i - 1], s2s_sem.at[i - 1], s2r_sem.at[i - 1], (at(i, 0), z))

    for i in (1, 3, 2, 0):
        for j in (1, 3, 2):
            k = i * 4 + j
            block_code(s1, (j - 1) * 4 + i, acc_own[k] + sib[k])
            go(first_copy(i, j))
    for i in (1, 3, 2, 0):
        k = i * 4
        value = acc_own[k] + sib[k]
        for j in (1, 3, 2):
            first_copy(i, j).wait_recv()
            value = value + block_decode(r1, (j - 1) * 4 + i)
        if i:
            block_code(s2, i - 1, value)
            go(second_copy(i))
    for i in (1, 3, 2):
        second_copy(i).wait_recv()
        value = value + block_decode(r2, i - 1)
    own = value.astype(BF16)
    hg[7] = own
    hg_out[...] = own

    def g_place(direction, step):
        return 7 if step < 0 else min(step * 2 + direction, 6)

    def g_copy(direction, step, half):
        k = unit_index(direction, step, half)
        rows = pl.ds(half * 64, 64)
        return remote(
            hg.at[g_place(direction, step - 1), rows],
            hg.at[g_place(direction, step), rows],
            gs_sem.at[k],
            gr_sem.at[k],
            (right, left)[direction],
        )

    def unit_part(place, chunk):
        cols = dw[:, pl.ds(pl.multiple_of(chunk * FEAT, FEAT), FEAT)]
        return lax.dot_general(hg[place], cols, (((1,), (1,)), ((), ())), preferred_element_type=F32)

    for half in (0, 1):
        for direction in (0, 1):
            go(g_copy(direction, 0, half))
    dw_copy.wait()
    unit[...] = unit_part(7, z)
    for step in (1, 2, 3):
        for half in (0, 1):
            for direction in (0, 1):
                h = half if direction == 0 else 1 - half
                g_copy(direction, step - 1, h).wait_recv()
                if step < 3 or h == direction:
                    go(g_copy(direction, step, h))
        for direction in (0, 1):
            unit[...] += unit_part(g_place(direction, step - 1), away(1 - direction, step))
    for direction in (0, 1):
        g_copy(direction, 3, direction).wait_recv()
    unit[...] += unit_part(6, away(0, 4))

    for k in range(HU // TILE):
        part = slice(k * TILE, (k + 1) * TILE)
        grad = unit[:, part]
        g = gate[:, part].astype(F32)
        u = up[:, part].astype(F32)
        sig = 1.0 / (1.0 + jnp.exp(-g))
        ug_out[:, part] = (grad * g * sig).astype(BF16)
        gg_out[:, part] = (grad * u * sig * (1.0 + g * (1.0 - sig))).astype(BF16)

    for copy in sends:
        copy.wait_send()


def on_device(hidden, head_weight, lse, targets, loss_weight, block_tiles, block_counts, gate_pre, up_pre, down_weight):
    vmem = pl.BlockSpec(memory_space=pltpu.VMEM)
    smem = pl.BlockSpec(memory_space=pltpu.SMEM)
    hbm = pl.BlockSpec(memory_space=pl.ANY)
    dma = pltpu.SemaphoreType.DMA
    return pl.pallas_call(
        body,
        out_shape=(
            jax.ShapeDtypeStruct((TILE, FEAT), BF16),
            jax.ShapeDtypeStruct((TILE, HU), BF16),
            jax.ShapeDtypeStruct((TILE, HU), BF16),
        ),
        in_specs=[hbm, hbm, vmem, vmem, vmem, smem, smem, vmem, vmem, hbm],
        out_specs=(vmem, vmem, vmem),
        scratch_shapes=[
            pltpu.VMEM((BLOCKS, TILE, FEAT), BF16),
            pltpu.VMEM((VT, TILE, FEAT), BF16),
            pltpu.VMEM((HU, Z * FEAT), BF16),
            pltpu.VMEM((SLOTS, TILE, TILE), F32),
            pltpu.VMEM((SLOTS + 1, TILE, TILE), BF16),
            pltpu.VMEM((16, TILE, FEAT), F32),
            pltpu.VMEM((16, TILE, FEAT), F32),
            pltpu.VMEM((16, TILE, FEAT), F32),
            pltpu.VMEM((16, UNIT, TILE), I16),
            pltpu.VMEM((16, UNIT, TILE), I16),
            pltpu.VMEM((12, TILE + 16, FEAT), I16),
            pltpu.VMEM((12, TILE + 16, FEAT), I16),
            pltpu.VMEM((3, TILE + 16, FEAT), I16),
            pltpu.VMEM((3, TILE + 16, FEAT), I16),
            pltpu.VMEM((Z, TILE, FEAT), BF16),
            pltpu.VMEM((TILE, HU), F32),
            pltpu.VMEM((BLOCKS, 8, TILE), F32),
            pltpu.VMEM((BLOCKS, 8, TILE), F32),
            pltpu.SMEM((BLOCKS + 1,), I32),
            pltpu.SMEM((SLOTS,), I32),
            pltpu.SMEM((SLOTS,), I32),
            dma((3,)),
            dma((31,)),
            dma((32,)),
            dma((16,)),
            dma((16,)),
            dma((16,)),
            dma((16,)),
            dma((16,)),
            dma((16,)),
            dma((12,)),
            dma((12,)),
            dma((3,)),
            dma((3,)),
            dma((16,)),
            dma((16,)),
        ],
        compiler_params=pltpu.CompilerParams(
            collective_id=0, has_side_effects=True, vmem_limit_bytes=60 * 2**20
        ),
        cost_estimate=pl.CostEstimate(flops=4 * 10**9, bytes_accessed=13 * 10**6, transcendentals=10**6),
    )(
        hidden,
        head_weight.reshape(VT, TILE, FEAT),
        lse.reshape(BLOCKS, TILE),
        targets.reshape(BLOCKS, TILE),
        loss_weight.reshape(BLOCKS, TILE),
        block_tiles,
        block_counts,
        gate_pre,
        up_pre,
        down_weight,
    )


def solution(mesh):
    in_specs = (
        P("wide", "narrow"),
        P("wide", "narrow"),
        P(),
        P(),
        P(),
        P(None, "wide", None),
        P(None, "wide"),
        P("wide", "narrow"),
        P("wide", "narrow"),
        P("narrow", None),
    )
    out_specs = (P("wide", "narrow"), P("wide", "narrow"), P("wide", "narrow"))
    return jax.shard_map(on_device, mesh=mesh, in_specs=in_specs, out_specs=out_specs, check_vma=False)
```

time: 382 us -> 139 us (0.36)
  waiting for transfers between devices: 226 us -> 0 us
  Pallas kernels: 0 us -> 131 us
  local copies, waits for them, and re-layouts: 57.4 us -> 7.56 us
  matrix products: 35.6 us -> 0 us
  blocking collectives: 34 us -> 0 us
  other arithmetic: 14.3 us -> 0 us
  between operations: 13.9 us -> 0.64 us
    reduce_scatter x2 -> x0, waiting for transfers between devices: 153 us -> none  [the longest x1 99.4 us: on_device(): lax.psum_scatter(softmax_part - factor[:, None] * target_rows, 'wide', sc...]
    pallas_call x0 -> x1, Pallas kernels: none -> 131 us  [on_device(): pl.pallas_call(body, out_shape=(jax.ShapeDtypeStruct((TILE, FEAT), BF16),...]
    all_gather x2 -> x0, waiting for transfers between devices: 71.8 us -> none  [the longest x1 46.3 us: on_device(): gathered = lax.all_gather(hidden, 'wide', axis=0, tiled=True)]
    gather x5 -> x0, local copies, waits for them, and re-layouts: 36.8 us -> none  [the longest x1 20.1 us: on_device(): jnp.take(head_weight, jnp.clip(local_ids, 0, vocab_here - 1), axis=0)]
    dot_general x4 -> x0, matrix products: 35.6 us -> none  [the longest x1 12.2 us: on_device(): jnp.dot(member, contrib, precision=lax.Precision.HIGHEST, preferred_eleme...]
    all_to_all x1 -> x0, blocking collectives: 34 us -> none  [sent_to_all(): return lax.all_to_all(copies, axis, split_axis=0, concat_axis=0, tiled=True)]
    sub x2 -> x0, other arithmetic: 9.93 us -> none  [the longest x1 9.83 us: on_device(): softmax_part - factor[:, None] * target_rows]
    reshape x1 -> x0, local copies, waits for them, and re-layouts: 7.48 us -> none  [on_device(): softmax_part = jnp.dot(member, contrib, precision=lax.Precision.HIGHEST,...]
  transfers between devices with their start and end apart: 4 -> 0, of which waited for: 4 -> 0; matrix products, arithmetic and copies ran while one was open for 8% -> 0% of each run, Pallas kernels for 0% -> 0%
where the time goes in v1:
time: 139 us
  Pallas kernels  131 us (94%)
  local copies, waits for them, and re-layouts  7.56 us (5%)
    pallas_call x1, Pallas kernels, on_device(): pl.pallas_call(body, out_shape=(jax.ShapeDtypeStruct((TILE, FEAT), BF16),...  131 us
    unnamed x5, local copies, waits for them, and re-layouts  7.56 us

profile of v1, /device:TPU:2, one launch (start us, length us, event | category | flops | bytes accessed | tf_op | source)
XLA Modules:
  0.0 138.7 jit_solution(933864635086659297)
XLA Ops:
  0.6 1.4 copy.13.tiles
  2.0 1.3 copy.14.counts
  3.3 130.5 %shard_map.121 = (bf16[128,512]{1,0:T(8,128)(2,1)}, bf16[128,896]{1,0:T(8,128)(2,1)}, bf16[128,896]{1,0:T(8,128)(2,1)}) custom-call(bf16[128,512]{1,0:T(8,128)(2,1)} %hidden.1, bf16[32,128,512]{2,1,0:T(8,128)(2,1)} %bitcast.4, f32[32,128]{1,0:T(8,128)} %bitcast.5, s32[32,128]{1,0:T(8,128)} %bitcast.6, f32[32,128]{1,0:T(8,128)} %bitcast.7, ...), custom_call_target="tpu_custom_call" | custom-call | flops 4000000000 | bytes 13000000 | tf_op jit(solution)/shard_map/pallas_call | solution.py:445
  133.9 1.6 %copy.18 = bf16[128,512]{1,0:T(8,128)(2,1)} copy(bf16[128,512]{1,0:T(8,128)(2,1)} %get-tuple-element.6) | data formatting | bytes 262144
  135.4 1.6 %copy.19 = bf16[128,896]{1,0:T(8,128)(2,1)} copy(bf16[128,896]{1,0:T(8,128)(2,1)} %get-tuple-element.7) | data formatting | bytes 458752
  137.1 1.6 %copy.20 = bf16[128,896]{1,0:T(8,128)(2,1)} copy(bf16[128,896]{1,0:T(8,128)(2,1)} %get-tuple-element.8) | data formatting | bytes 458752

commit v2 on v1

--- a/solution.py
+++ b/solution.py
@@ -44,8 +44,8 @@
     lse,
     targets,
     scale,
-    tiles,
-    counts,
+    tiles_in,
+    counts_in,
     gate,
     up,
     down,
@@ -70,6 +70,8 @@
     unit,
     lse_rows,
     scale_rows,
+    tiles,
+    counts,
     pos,
     slot_block,
     slot_tile,
@@ -118,6 +120,10 @@
     w_copy.start()
     dw_copy = pltpu.make_async_copy(down, dw, local_sem.at[2])
     dw_copy.start()
+    tiles_copy = pltpu.make_async_copy(tiles_in, tiles, local_sem.at[3])
+    tiles_copy.start()
+    counts_copy = pltpu.make_async_copy(counts_in, counts, local_sem.at[4])
+    counts_copy.start()
 
     barrier = pltpu.get_barrier_semaphore()
     peers = [sibling, right, left]
@@ -147,8 +153,6 @@
     def prefix(b, run):
         pos[b] = run
         return run + counts[b, 0]
-
-    pos[BLOCKS] = lax.fori_loop(0, BLOCKS, prefix, jnp.int32(0))
 
     def fill(s, carry):
         before = jnp.int32(0)
@@ -184,19 +188,22 @@
 
         lax.fori_loop(lo // 2, hi // 2, pair, 0)
 
+    for i in (1, 3, 2):
+        b = at(i, 0)
+        block_wait(b)
+        for j in (1, 3, 2):
+            block_send(hid.at[b], b, 2 + i * 3 + j, (at(0, j), z))
+        block_send(hid.at[b], b, 15 + i, sibling)
+    tiles_copy.wait()
+    counts_copy.wait()
+    pos[BLOCKS] = lax.fori_loop(0, BLOCKS, prefix, jnp.int32(0))
     lax.fori_loop(0, SLOTS, fill, 0)
     for b in range(BLOCKS):
         lse_rows[b] = jnp.broadcast_to(lse[b : b + 1, :], (8, TILE))
         scale_rows[b] = jnp.broadcast_to(scale[b : b + 1, :], (8, TILE))
     probs[SLOTS] = jnp.zeros((TILE, TILE), BF16)
     w_copy.wait()
-    for i in (1, 3, 2):
-        b = at(i, 0)
-        block_wait(b)
-        for j in (1, 3, 2):
-            block_send(hid.at[b], b, 2 + i * 3 + j, (at(0, j), z))
-        block_send(hid.at[b], b, 15 + i, sibling)
-        target_blocks((i - 1) * 2, i * 2)
+    target_blocks(0, 6)
     for j in (1, 3, 2):
         for i in (0, 1, 3, 2):
             b = at(i, j)
@@ -335,21 +342,21 @@
     def sib_copy(k):
         return remote(acc_sib.at[k], sib.at[k], bs_sem.at[k], br_sem.at[k], sibling)
 
-    def for_sibling(k, carry):
-        contribution(acc_sib, k, placed(k // 4, k % 4, 1 - c))
-        return carry
-
-    lax.fori_loop(0, 16, for_sibling, 0)
-    for k in range(16):
-        go(sib_copy(k))
-
-    def for_own(k, carry):
-        contribution(acc_own, k, placed(k // 4, k % 4, c))
-        return carry
-
-    lax.fori_loop(0, 16, for_own, 0)
-    for k in range(16):
-        sib_copy(k).wait_recv()
+    def group_for_sibling(i):
+        def one(k, carry):
+            contribution(acc_sib, k, placed(k // 4, k % 4, 1 - c))
+            return carry
+
+        lax.fori_loop(i * 4, i * 4 + 4, one, 0)
+        for j in range(4):
+            go(sib_copy(i * 4 + j))
+
+    def group_own(i):
+        def one(k, carry):
+            contribution(acc_own, k, placed(k // 4, k % 4, c))
+            return carry
+
+        lax.fori_loop(i * 4, i * 4 + 4, one, 0)
 
     def block_code(dst, k, value):
         e = scale_exponent(jnp.max(jnp.abs(value), axis=0, keepdims=True))
@@ -367,13 +374,28 @@
     def second_copy(i):
         return remote(s2.at[i - 1], r2.at[i - 1], s2s_sem.at[i - 1], s2r_sem.at[i - 1], (at(i, 0), z))
 
-    for i in (1, 3, 2, 0):
+    def group_send(i):
         for j in (1, 3, 2):
             k = i * 4 + j
+            sib_copy(k).wait_recv()
             block_code(s1, (j - 1) * 4 + i, acc_own[k] + sib[k])
             go(first_copy(i, j))
+
+    group_for_sibling(1)
+    group_for_sibling(3)
+    group_own(1)
+    group_send(1)
+    group_for_sibling(2)
+    group_own(3)
+    group_send(3)
+    group_for_sibling(0)
+    group_own(2)
+    group_send(2)
+    group_own(0)
+    group_send(0)
     for i in (1, 3, 2, 0):
         k = i * 4
+        sib_copy(k).wait_recv()
         value = acc_own[k] + sib[k]
         for j in (1, 3, 2):
             first_copy(i, j).wait_recv()
@@ -439,7 +461,6 @@
 
 def on_device(hidden, head_weight, lse, targets, loss_weight, block_tiles, block_counts, gate_pre, up_pre, down_weight):
     vmem = pl.BlockSpec(memory_space=pltpu.VMEM)
-    smem = pl.BlockSpec(memory_space=pltpu.SMEM)
     hbm = pl.BlockSpec(memory_space=pl.ANY)
     dma = pltpu.SemaphoreType.DMA
     return pl.pallas_call(
@@ -449,7 +470,7 @@
             jax.ShapeDtypeStruct((TILE, HU), BF16),
             jax.ShapeDtypeStruct((TILE, HU), BF16),
         ),
-        in_specs=[hbm, hbm, vmem, vmem, vmem, smem, smem, vmem, vmem, hbm],
+        in_specs=[hbm, hbm, vmem, vmem, vmem, hbm, hbm, vmem, vmem, hbm],
         out_specs=(vmem, vmem, vmem),
         scratch_shapes=[
             pltpu.VMEM((BLOCKS, TILE, FEAT), BF16),
@@ -470,10 +491,12 @@
             pltpu.VMEM((TILE, HU), F32),
             pltpu.VMEM((BLOCKS, 8, TILE), F32),
             pltpu.VMEM((BLOCKS, 8, TILE), F32),
+            pltpu.SMEM((BLOCKS, 1, MAXT), I32),
+            pltpu.SMEM((BLOCKS, 1), I32),
             pltpu.SMEM((BLOCKS + 1,), I32),
             pltpu.SMEM((SLOTS,), I32),
             pltpu.SMEM((SLOTS,), I32),
-            dma((3,)),
+            dma((5,)),
             dma((31,)),
             dma((32,)),
             dma((16,)),

time: 139 us -> 133 us (0.957); the launches traced: 139 us -> 131 us
  Pallas kernels: 131 us -> 122 us
    pallas_call x1, Pallas kernels: 131 us -> 122 us  [on_device(): pl.pallas_call(body, out_shape=(jax.ShapeDtypeStruct((TILE, FEAT), BF16),...]
where the time goes in v2:
time: 133 us; the launch traced here: 131 us
  Pallas kernels  122 us (92%)
  local copies, waits for them, and re-layouts  7.56 us (6%)
    pallas_call x1, Pallas kernels, on_device(): pl.pallas_call(body, out_shape=(jax.ShapeDtypeStruct((TILE, FEAT), BF16),...  122 us
    unnamed x5, local copies, waits for them, and re-layouts  7.56 us

profile of v2, /device:TPU:2, one launch (start us, length us, event | category | flops | bytes accessed | tf_op | source)
XLA Modules:
  0.0 130.7 jit_solution(17759219135364726633)
XLA Ops:
  0.6 1.4 %copy.13.tiles_in = s32[32,1,4]{2,1,0:T(1,128)} copy(s32[32,1,4]{0,2,1:T(4,128)} %param.15) | data formatting | bytes 1024 | tf_op args[5]
  2.0 1.3 %copy.14.counts_in = s32[32,1]{1,0:T(8,128)} copy(s32[32,1]{0,1:T(1,128)} %param.16) | data formatting | bytes 256 | tf_op args[6]
  3.3 122.5 %shard_map.121 = (bf16[128,512]{1,0:T(8,128)(2,1)}, bf16[128,896]{1,0:T(8,128)(2,1)}, bf16[128,896]{1,0:T(8,128)(2,1)}) custom-call(bf16[128,512]{1,0:T(8,128)(2,1)} %hidden.1, bf16[32,128,512]{2,1,0:T(8,128)(2,1)} %bitcast.4, f32[32,128]{1,0:T(8,128)} %bitcast.5, s32[32,128]{1,0:T(8,128)} %bitcast.6, f32[32,128]{1,0:T(8,128)} %bitcast.7, ...), custom_call_target="tpu_custom_call" | custom-call | flops 4000000000 | bytes 13000000 | tf_op jit(solution)/shard_map/pallas_call | solution.py:466
  125.8 1.6 %copy.18 = bf16[128,512]{1,0:T(8,128)(2,1)} copy(bf16[128,512]{1,0:T(8,128)(2,1)} %get-tuple-element.6) | data formatting | bytes 262144
  127.4 1.6 %copy.19 = bf16[128,896]{1,0:T(8,128)(2,1)} copy(bf16[128,896]{1,0:T(8,128)(2,1)} %get-tuple-element.7) | data formatting | bytes 458752
  129.0 1.6 %copy.20 = bf16[128,896]{1,0:T(8,128)(2,1)} copy(bf16[128,896]{1,0:T(8,128)(2,1)} %get-tuple-element.8) | data formatting | bytes 458752

commit v3 on v2

--- a/solution.py
+++ b/solution.py
@@ -68,6 +68,8 @@
     r2,
     hg,
     unit,
+    up_factor,
+    gate_factor,
     lse_rows,
     scale_rows,
     tiles,
@@ -152,7 +154,7 @@
 
     def prefix(b, run):
         pos[b] = run
-        return run + counts[b, 0]
+        return run + counts[0, b]
 
     def fill(s, carry):
         before = jnp.int32(0)
@@ -161,7 +163,7 @@
         b = jnp.minimum(before, BLOCKS - 1)
         j = jnp.clip(s - pos[b], 0, MAXT - 1)
         slot_block[s] = b
-        slot_tile[s] = jnp.clip(tiles[b, 0, j], 0, VT - 1)
+        slot_tile[s] = jnp.clip(tiles[j, b], 0, VT - 1)
         return carry
 
     lane = lax.broadcasted_iota(I32, (TILE, TILE), 1)
@@ -239,7 +241,7 @@
             zs[k, pl.ds(pl.multiple_of(i * TILE, TILE), TILE), :] = code(value, e)
             return jnp.where(row16 == i, e, exps)
 
-        exps = lax.fori_loop(0, HALF, slot, jnp.zeros((16, TILE), F32))
+        exps = lax.fori_loop(0, HALF, slot, jnp.zeros((16, TILE), F32), unroll=2)
         zs[k, HALF * TILE : UNIT, :] = exps.astype(I32).astype(I16)
 
     def unit_index(direction, step, half):
@@ -256,6 +258,14 @@
 
     def away(direction, distance):
         return (z + (distance if direction == 0 else Z - distance)) % Z
+
+    def gate_factors():
+        for k in range(HU // TILE):
+            part = slice(k * TILE, (k + 1) * TILE)
+            g = gate[:, part].astype(F32)
+            sig = 1.0 / (1.0 + jnp.exp(-g))
+            up_factor[:, part] = g * sig
+            gate_factor[:, part] = up[:, part].astype(F32) * sig * (1.0 + g * (1.0 - sig))
 
     logits(away(0, 4))
     for direction in (0, 1):
@@ -271,17 +281,18 @@
     for step in (1, 2, 3):
         for half in (0, 1):
             for direction in (0, 1):
-                h = half if direction == 0 else 1 - half
-                if step == 1 and h != direction:
+                if step == 1 and half != direction:
                     continue
-                k = unit_wait(direction, step - 1, h)
-                unit_code(unit_index(direction, step, h), away(direction, 4 - step), h, k)
-                unit_send(direction, step, h)
+                k = unit_wait(direction, step - 1, half)
+                unit_code(unit_index(direction, step, half), away(direction, 4 - step), half, k)
+                unit_send(direction, step, half)
         if step == 1:
             logits(away(0, 1))
             logits(away(1, 1))
             logits(z)
         target_blocks(4 + step * 2, 6 + step * 2)
+        if step == 2:
+            gate_factors()
 
     def part_refs(t, chunk, half):
         return probs.at[pl.ds(chunk * 8 + half * HALF, HALF)]
@@ -313,17 +324,16 @@
             probs[s] = value.T.astype(BF16)
             return carry
 
-        lax.fori_loop(0, HALF, prob_slot, 0)
+        lax.fori_loop(0, HALF, prob_slot, 0, unroll=2)
         for direction in (0, 1):
             p_send(direction, 0, half)
     target_blocks(12, 16)
     for step in (1, 2, 3):
         for half in (0, 1):
             for direction in (0, 1):
-                h = half if direction == 0 else 1 - half
-                p_wait(direction, step - 1, h)
-                if step < 3 or h == direction:
-                    p_send(direction, step, h)
+                p_wait(direction, step - 1, half)
+                if step < 3 or half == direction:
+                    p_send(direction, step, half)
         target_blocks(12 + step * 4, 16 + step * 4)
     target_blocks(28, 32)
     for direction in (0, 1):
@@ -332,9 +342,9 @@
     def contribution(acc, k, b):
         taken, entries = [], []
         for j in range(MAXT):
-            live = jnp.clip(counts[b, 0] - j, 0, 1)
+            live = jnp.clip(counts[0, b] - j, 0, 1)
             taken.append(probs[jnp.clip(live * (pos[b] + j) + (1 - live) * SLOTS, 0, SLOTS)])
-            entries.append(w[jnp.clip(tiles[b, 0, j], 0, VT - 1)])
+            entries.append(w[jnp.clip(tiles[j, b], 0, VT - 1)])
         acc[k] = acc[k] + jnp.dot(
             jnp.concatenate(taken, axis=1), jnp.concatenate(entries, axis=0), preferred_element_type=F32
         )
@@ -347,7 +357,7 @@
             contribution(acc_sib, k, placed(k // 4, k % 4, 1 - c))
             return carry
 
-        lax.fori_loop(i * 4, i * 4 + 4, one, 0)
+        lax.fori_loop(i * 4, i * 4 + 4, one, 0, unroll=2)
         for j in range(4):
             go(sib_copy(i * 4 + j))
 
@@ -356,7 +366,7 @@
             contribution(acc_own, k, placed(k // 4, k % 4, c))
             return carry
 
-        lax.fori_loop(i * 4, i * 4 + 4, one, 0)
+        lax.fori_loop(i * 4, i * 4 + 4, one, 0, unroll=2)
 
     def block_code(dst, k, value):
         e = scale_exponent(jnp.max(jnp.abs(value), axis=0, keepdims=True))
@@ -436,10 +446,9 @@
     for step in (1, 2, 3):
         for half in (0, 1):
             for direction in (0, 1):
-                h = half if direction == 0 else 1 - half
-                g_copy(direction, step - 1, h).wait_recv()
-                if step < 3 or h == direction:
-                    go(g_copy(direction, step, h))
+                g_copy(direction, step - 1, half).wait_recv()
+                if step < 3 or half == direction:
+                    go(g_copy(direction, step, half))
         for direction in (0, 1):
             unit[...] += unit_part(g_place(direction, step - 1), away(1 - direction, step))
     for direction in (0, 1):
@@ -449,11 +458,8 @@
     for k in range(HU // TILE):
         part = slice(k * TILE, (k + 1) * TILE)
         grad = unit[:, part]
-        g = gate[:, part].astype(F32)
-        u = up[:, part].astype(F32)
-        sig = 1.0 / (1.0 + jnp.exp(-g))
-        ug_out[:, part] = (grad * g * sig).astype(BF16)
-        gg_out[:, part] = (grad * u * sig * (1.0 + g * (1.0 - sig))).astype(BF16)
+        ug_out[:, part] = (grad * up_factor[:, part]).astype(BF16)
+        gg_out[:, part] = (grad * gate_factor[:, part]).astype(BF16)
 
     for copy in sends:
         copy.wait_send()
@@ -489,10 +495,12 @@
             pltpu.VMEM((3, TILE + 16, FEAT), I16),
             pltpu.VMEM((Z, TILE, FEAT), BF16),
             pltpu.VMEM((TILE, HU), F32),
+            pltpu.VMEM((TILE, HU), F32),
+            pltpu.VMEM((TILE, HU), F32),
             pltpu.VMEM((BLOCKS, 8, TILE), F32),
             pltpu.VMEM((BLOCKS, 8, TILE), F32),
-            pltpu.SMEM((BLOCKS, 1, MAXT), I32),
-            pltpu.SMEM((BLOCKS, 1), I32),
+            pltpu.SMEM((MAXT, BLOCKS), I32),
+            pltpu.SMEM((1, BLOCKS), I32),
             pltpu.SMEM((BLOCKS + 1,), I32),
             pltpu.SMEM((SLOTS,), I32),
             pltpu.SMEM((SLOTS,), I32),
@@ -522,8 +530,8 @@
         lse.reshape(BLOCKS, TILE),
         targets.reshape(BLOCKS, TILE),
         loss_weight.reshape(BLOCKS, TILE),
-        block_tiles,
-        block_counts,
+        block_tiles[:, 0, :].T,
+        block_counts.T,
         gate_pre,
         up_pre,
         down_weight,

time: 133 us -> 125 us (0.940)
  Pallas kernels: 122 us -> 118 us
  local copies, waits for them, and re-layouts: 7.56 us -> 4.86 us
    pallas_call x1, Pallas kernels: 122 us -> 118 us  [on_device(): pl.pallas_call(body, out_shape=(jax.ShapeDtypeStruct((TILE, FEAT), BF16),...]
    unnamed x5 -> x3, local copies, waits for them, and re-layouts: 7.56 us -> 4.86 us
where the time goes in v3:
time: 125 us; the launch traced here: 123 us
  Pallas kernels  118 us (94%)
  local copies, waits for them, and re-layouts  4.86 us (4%)
    pallas_call x1, Pallas kernels, on_device(): pl.pallas_call(body, out_shape=(jax.ShapeDtypeStruct((TILE, FEAT), BF16),...  118 us
    unnamed x3, local copies, waits for them, and re-layouts  4.86 us

profile of v3, /device:TPU:2, one launch (start us, length us, event | category | flops | bytes accessed | tf_op | source)
XLA Modules:
  0.0 123.3 jit_solution(2209483827626100424)
XLA Ops:
  0.6 117.8 %shard_map.121 = (bf16[128,512]{1,0:T(8,128)(2,1)}, bf16[128,896]{1,0:T(8,128)(2,1)}, bf16[128,896]{1,0:T(8,128)(2,1)}) custom-call(bf16[128,512]{1,0:T(8,128)(2,1)} %hidden.1, bf16[32,128,512]{2,1,0:T(8,128)(2,1)} %bitcast.8, f32[32,128]{1,0:T(8,128)} %bitcast.9, s32[32,128]{1,0:T(8,128)} %bitcast.10, f32[32,128]{1,0:T(8,128)} %bitcast.11, ...), custom_call_target="tpu_custom_call" | custom-call | flops 4000000000 | bytes 13000000 | tf_op jit(solution)/shard_map/pallas_call | solution.py:472
  118.4 1.6 %copy.16 = bf16[128,512]{1,0:T(8,128)(2,1)} copy(bf16[128,512]{1,0:T(8,128)(2,1)} %get-tuple-element.6) | data formatting | bytes 262144
  120.0 1.6 %copy.17 = bf16[128,896]{1,0:T(8,128)(2,1)} copy(bf16[128,896]{1,0:T(8,128)(2,1)} %get-tuple-element.7) | data formatting | bytes 458752
  121.6 1.6 %copy.18 = bf16[128,896]{1,0:T(8,128)(2,1)} copy(bf16[128,896]{1,0:T(8,128)(2,1)} %get-tuple-element.8) | data formatting | bytes 458752
